TPU v7x, 32 devices: a whole 2x2x4 slice. The times are simulated.
32 devices in a mesh: member: 2 (over x), lat: 16 (over z, y, core).
Axes of the slice: x: 2, y: 2, z: 4, core: 2. Of those that a mesh axis runs over, the one named last changes fastest.
Arguments:
- state: float32 [10, 128, 128, 256], P('member', None, 'lat'), parts along dimension 0, may hold values from -6 to 6
- wind: float32 [256, 128, 256], P('member', 'lat'), parts along dimension 0, may hold values from -0.9 to 0.9
- sunlight: float32 [256, 256], P(('member', 'lat')), parts along dimension 0, may hold values from 0.1 to 1
- day_list: int32 [32, 16], P(('member', 'lat')), parts along dimension 0, may hold values from -1 to 15, as said below
- w_first: bfloat16 [640, 2048], replicated, may hold values from -0.25 to 0.25
- bias: float32 [2048], replicated, may hold values from -3 to 3
- w_second: bfloat16 [2048, 128], replicated, may hold values from -0.125 to 0.125
- remap: float32 [128, 128], replicated, may hold values from -1.5 to 2
Outputs:
- new_state: float32 [10, 128, 128, 256], P('member', None, 'lat'), parts along dimension 0
There are 2 independent parts, one for each index of `member`. A program takes and returns all parts, laid end to end along the dimension named above; an argument that names none is the same for every part. Nothing has to cross between parts.
Inputs may be any that keep to these rules, and one draw needn't show every extreme that they name: `day_list`: row d names the daylit blocks of band d, each once, as a cyclic run of consecutive numbers placed first, then -1; every row names at least one block. Rows d and d + 8 together name at most 20 blocks; row 0 names all 16 and row 8 exactly 4.
All inputs are finite; a program needn't handle non-finite values.
Results may differ from a plain program's by a relative error of at most 0.00062.
Values may be sent and summed in bfloat16 or wider, within the bound.
A program may use at most 128 MiB of HBM per device.

v0:
```python
import jax
import jax.numpy as jnp
from jax import lax
from jax.sharding import PartitionSpec as P

STEPS = 2


def shifted(block, axis, distance):
    devices = range(lax.axis_size(axis))
    route = [(i - distance, i) for i in devices if i - distance in devices]
    return lax.ppermute(block, axis, route)


def padded_2(x, sides, width):
    for axis, dim in sides:
        count, length = (lax.axis_size(axis), x.shape[dim])
        up = [(i, (i + 1) % count) for i in range(count - 1)]
        down = [(j, i) for i, j in up]
        last = lax.slice_in_dim(x, length - width, length, axis=dim)
        leading = lax.slice_in_dim(x, 0, width, axis=dim)
        before = lax.ppermute(last, axis, up)
        after = lax.ppermute(leading, axis, down)
        x = jnp.concatenate([before, x, after], axis=dim)
    return x


def min_mod(left, right):
    return 0.5 * (jnp.sign(left) + jnp.sign(right)) * jnp.minimum(jnp.abs(left), jnp.abs(right))


def advance(padded, courant):
    length = padded.shape[2] - 4
    slopes = min_mod(padded[:, :, 2:] - padded[:, :, 1:-1], padded[:, :, 1:-1] - padded[:, :, :-2])
    upper_q = padded[:, :, 1 : length + 2]
    upper_s = slopes[:, :, 0 : length + 1]
    lower_q = padded[:, :, 2 : length + 3]
    lower_s = slopes[:, :, 1 : length + 2]
    speed = courant[None]
    fluxes = jnp.where(
        speed > 0.0,
        speed * (upper_q + 0.5 * (1.0 - speed) * upper_s),
        speed * (lower_q - 0.5 * (1.0 + speed) * lower_s),
    )
    return padded[:, :, 2 : length + 2] - (fluxes[:, :, 1:] - fluxes[:, :, :-1])


def radiate(sources, slot_index, w_shaped, bias, w_second):
    picked = jnp.take(sources, slot_index, axis=2)
    hidden = (
        jnp.einsum("flkc,flh->kch", picked, w_shaped, preferred_element_type=jnp.float32) + bias
    )
    hidden = jax.nn.gelu(hidden, approximate=True).astype(jnp.bfloat16)
    return jnp.einsum("kch,hl->klc", hidden, w_second, preferred_element_type=jnp.float32)


def place_blocks(listed, results, block_ids):
    owner = (listed[None, :] == block_ids[:, None]).astype(jnp.float32)
    return jnp.einsum("bs,slc->lbc", owner, results, precision=lax.Precision.HIGHEST)


def shards(state, wind, sunlight, day_list, w_first, bias, w_second, remap):
    fields, levels, rows, lons = state.shape
    next_row = shifted(wind[:, :1, :], "lat", -1)
    courant = jnp.concatenate([wind, next_row], axis=1)
    current = state
    for step in range(STEPS):
        padded = padded_2(current, (("lat", 2),), 2)
        current = advance(padded, courant)
    columns = current.reshape(fields, levels, rows * lons)
    remapped = jnp.einsum("km,fmc->fkc", remap, columns, precision=lax.Precision.HIGHEST)
    blocks = day_list.shape[1]
    block_width = rows * lons // blocks
    inputs = remapped.astype(jnp.bfloat16).reshape(fields, levels, blocks, block_width)
    w_shaped = w_first.reshape(fields, levels, w_first.shape[1])
    listed = day_list[0]
    block_ids = jnp.arange(blocks, dtype=jnp.int32)
    safe_ids = jnp.maximum(listed, 0)
    results = radiate(inputs, safe_ids, w_shaped, bias, w_second)
    heating = place_blocks(listed, results, block_ids)
    heating = heating.reshape(levels, rows * lons) * sunlight.reshape(1, rows * lons)
    output = jnp.concatenate([remapped[:1] + heating[None], remapped[1:]], axis=0)
    return output.reshape(fields, levels, rows, lons)


def solution(mesh):
    placed = (
        P("member", None, "lat", None),
        P("member", "lat", None),
        P(("member", "lat"), None),
        P(("member", "lat"), None),
        P(),
        P(),
        P(),
        P(),
    )
    return jax.shard_map(
        shards,
        mesh=mesh,
        in_specs=placed,
        out_specs=P("member", None, "lat", None),
        check_vma=False,
    )
```

profile of v0, /device:TPU:20, one launch (start us, length us, event | category | flops | bytes accessed | tf_op | source)
XLA Modules:
  0.0 197.0 jit_solution(10704786735371431547)
XLA Ops:
  0.0 0.0 copy-start
  0.0 5.2 %fusion.57 = (f32[5,128,2,256]{3,2,1,0:T(2,128)S(1)}, f32[5,128,2,256]{3,2,1,0:T(2,128)S(1)}) fusion(f32[5,128,8,256]{3,2,1,0:T(8,128)} %param.8), kind=kLoop, calls=%fused_computation.86 | loop fusion | bytes 5242880 | tf_op jit(solution)/shard_map/slice | solution.py:20
  5.2 1.2 copy.77
  6.4 1.9 collective-permute-start.1
  8.3 1.2 copy.78
  9.5 3.6 %collective-permute-start.2 = (f32[5,128,2,256]{3,1,2,0:T(8,128)}, f32[5,128,2,256]{3,1,2,0:T(8,128)}, u32[]{:S(2)}, u32[]{:S(2)}) collective-permute-start(f32[5,128,2,256]{3,1,2,0:T(8,128)} %copy.78), channel_id=1, source_target_pairs={{1,0},{2,1},{3,2},{4,3},{5,4},{6,5},{7,6},{8,7},{9,8},{10,9},{11,1... | collective-permute-start | bytes 3932168 | tf_op jit(solution)/shard_map/ppermute | solution.py:23
  13.2 0.0 slice-done.4
  13.2 1.9 collective-permute-start
  15.1 0.0 copy-done.3
  15.2 1.4 constant_dynamic-update-slice_fusion.1
  16.5 6.1 %copy.66 = f32[5,128,8,256]{1,3,2,0:T(8,128)} copy(f32[5,128,8,256]{3,2,1,0:T(8,128)} %param.8) | data formatting | bytes 10485760 | tf_op args[0]
  22.6 17.3 %collective-permute-done = f32[128,1,256]{2,0,1:T(8,128)S(1)} collective-permute-done((f32[128,1,256]{2,0,1:T(8,128)S(1)}, f32[128,1,256]{2,0,1:T(8,128)S(1)}, u32[]{:S(2)}, u32[]{:S(2)}) %collective-permute-start) | collective-permute-done | bytes 131104 | tf_op jit(solution)/shard_map/ppermute | solution.py:12
  39.9 0.6 constant_dynamic-update-slice_fusion
  40.6 2.7 %copy.54 = f32[128,9,256]{0,2,1:T(8,128)} copy(f32[128,9,256]{2,0,1:T(8,128)} %constant_dynamic-update-slice_fusion) | data formatting | bytes 2359296 | tf_op jit(solution)/shard_map/concatenate | solution.py:65
  43.2 2.9 %subtract_multiply_fusion = (f32[128,9,256]{2,0,1:T(8,128)}, f32[128,9,256]{2,0,1:T(8,128)}) fusion(f32[128,9,256]{2,0,1:T(8,128)} %constant_dynamic-update-slice_fusion), kind=kLoop, calls=%fused_computation.66 | loop fusion | flops 1179648 | bytes 3538944 | tf_op jit(solution)/shard_map/mul | solution.py:42
  46.2 2.6 %copy.58 = f32[128,9,256]{0,2,1:T(8,128)} copy(f32[128,9,256]{2,0,1:T(8,128)} %get-tuple-element.9) | data formatting | bytes 2359296 | tf_op jit(solution)/shard_map/mul | solution.py:42
  48.8 2.6 %copy.65 = f32[128,9,256]{0,2,1:T(8,128)} copy(f32[128,9,256]{2,0,1:T(8,128)} %get-tuple-element.10) | data formatting | bytes 2359296 | tf_op jit(solution)/shard_map/mul | solution.py:43
  51.5 1.4 broadcast_compare_fusion
  52.9 1.1 copy.53
  54.0 0.0 collective-permute-done.1
  54.0 2.8 %copy.56 = f32[5,128,2,256]{1,3,2,0:T(8,128)} copy(f32[5,128,2,256]{3,1,2,0:T(8,128)} %collective-permute-done.1) | data formatting | bytes 2621440 | tf_op jit(solution)/shard_map/ppermute | solution.py:22
  56.8 0.0 collective-permute-done.2
  56.8 2.9 %copy.61 = f32[5,128,2,256]{1,3,2,0:T(8,128)} copy(f32[5,128,2,256]{3,1,2,0:T(8,128)} %collective-permute-done.2) | data formatting | bytes 2621440 | tf_op jit(solution)/shard_map/ppermute | solution.py:23
  59.7 9.1 %minimum_multiply_fusion.1 = f32[5,128,10,256]{1,3,2,0:T(8,128)S(1)} fusion(f32[5,128,8,256]{1,3,2,0:T(8,128)} %copy.66, f32[5,128,2,256]{1,3,2,0:T(8,128)} %copy.56, f32[5,128,2,256]{1,3,2,0:T(8,128)} %copy.61), kind=kLoop, calls=%fused_computation.33 | loop fusion | flops 22937600 | bytes 14417920 | tf_op jit(solution)/shard_map/mul | solution.py:29
  68.8 0.0 slice-start.3
  68.8 8.7 %fusion.24 = f32[5,128,9,256]{1,3,2,0:T(8,128)} fusion(f32[5,128,8,256]{1,3,2,0:T(8,128)} %copy.66, f32[5,128,2,256]{1,3,2,0:T(8,128)} %copy.61, f32[5,128,2,256]{1,3,2,0:T(8,128)} %copy.56, f32[5,128,10,256]{1,3,2,0:T(8,128)S(1)} %minimum_multiply_fusion.1, f32[128,9,256]{0,2,1:T(8,128)} %copy.65, f32[128,9,256]{0,2,1:T(8,128)} %copy.58, ...), kind=kLoop, calls=%fused_computation.44 | loop fusion | flops 13271040 | bytes 29392896 | tf_op jit(solution)/shard_map/jit(_where)/select_n | solution.py:40
  77.5 0.0 slice-done.2
  77.5 0.0 slice-done.3
  77.5 5.5 %fusion.29 = f32[5,128,8,256]{1,3,2,0:T(8,128)S(1)} fusion(f32[5,128,8,256]{1,3,2,0:T(8,128)S(1)} %bitcast.54, f32[5,128,9,256]{1,3,2,0:T(8,128)} %fusion.24), kind=kLoop, calls=%fused_computation.55 | loop fusion | flops 2621440 | bytes 20971520 | tf_op jit(solution)/shard_map/sub | solution.py:45
  83.0 0.0 copy-start.1
  83.0 2.3 %copy-done.1 = f32[5,128,8,256]{1,3,2,0:T(8,128)} copy-done((f32[5,128,8,256]{1,3,2,0:T(8,128)}, f32[5,128,8,256]{1,3,2,0:T(8,128)S(1)}, u32[]{:S(2)}) %copy-start.1) | copy-done | bytes 5242904
  85.3 1.7 fusion.56
  87.0 2.8 %copy.67 = f32[5,128,2,256]{3,1,2,0:T(8,128)} copy(f32[5,128,2,256]{1,3,2,0:T(8,128)} %get-tuple-element.5) | data formatting | bytes 2621440 | tf_op jit(solution)/shard_map/slice | solution.py:20
  89.8 1.9 collective-permute-start.3
  91.8 2.8 %copy.69 = f32[5,128,2,256]{3,1,2,0:T(8,128)} copy(f32[5,128,2,256]{1,3,2,0:T(8,128)} %get-tuple-element.6) | data formatting | bytes 2621440 | tf_op jit(solution)/shard_map/slice | solution.py:21
  94.5 4.0 %collective-permute-start.4 = (f32[5,128,2,256]{3,1,2,0:T(8,128)}, f32[5,128,2,256]{3,1,2,0:T(8,128)}, u32[]{:S(2)}, u32[]{:S(2)}) collective-permute-start(f32[5,128,2,256]{3,1,2,0:T(8,128)} %copy.69), channel_id=1, source_target_pairs={{1,0},{2,1},{3,2},{4,3},{5,4},{6,5},{7,6},{8,7},{9,8},{10,9},{11,1... | collective-permute-start | bytes 3932168 | tf_op jit(solution)/shard_map/ppermute | solution.py:23
  98.5 0.0 copy-done.5
  98.6 0.0 copy-done.6
  98.6 24.7 %collective-permute-done.3 = f32[5,128,2,256]{3,1,2,0:T(8,128)} collective-permute-done((f32[5,128,2,256]{3,1,2,0:T(8,128)}, f32[5,128,2,256]{3,1,2,0:T(8,128)}, u32[]{:S(2)}, u32[]{:S(2)}) %collective-permute-start.3) | collective-permute-done | bytes 1310752 | tf_op jit(solution)/shard_map/ppermute | solution.py:22
  123.3 2.8 %copy.68 = f32[5,128,2,256]{1,3,2,0:T(8,128)} copy(f32[5,128,2,256]{3,1,2,0:T(8,128)} %collective-permute-done.3) | data formatting | bytes 2621440 | tf_op jit(solution)/shard_map/ppermute | solution.py:22
  126.1 0.0 collective-permute-done.4
  126.1 2.9 %copy.70 = f32[5,128,2,256]{1,3,2,0:T(8,128)} copy(f32[5,128,2,256]{3,1,2,0:T(8,128)} %collective-permute-done.4) | data formatting | bytes 2621440 | tf_op jit(solution)/shard_map/ppermute | solution.py:23
  129.0 9.1 %minimum_multiply_fusion = f32[5,128,10,256]{1,3,2,0:T(8,128)S(1)} fusion(f32[5,128,8,256]{1,3,2,0:T(8,128)} %copy-done.1, f32[5,128,2,256]{1,3,2,0:T(8,128)} %copy.68, f32[5,128,2,256]{1,3,2,0:T(8,128)} %copy.70), kind=kLoop, calls=%fused_computation.32 | loop fusion | flops 22937600 | bytes 14417920 | tf_op jit(solution)/shard_map/mul | solution.py:29
  138.1 0.0 slice-start.1
  138.1 8.7 %fusion.17 = f32[5,128,9,256]{1,3,2,0:T(8,128)} fusion(f32[5,128,8,256]{1,3,2,0:T(8,128)} %copy-done.1, f32[5,128,2,256]{1,3,2,0:T(8,128)} %copy.70, f32[5,128,2,256]{1,3,2,0:T(8,128)} %copy.68, f32[5,128,10,256]{1,3,2,0:T(8,128)S(1)} %minimum_multiply_fusion, f32[128,9,256]{0,2,1:T(8,128)} %copy.65, f32[128,9,256]{0,2,1:T(8,128)} %copy.58, ...), kind=kLoop, calls=%fused_computation.37 | loop fusion | flops 13271040 | bytes 29392896 | tf_op jit(solution)/shard_map/jit(_where)/select_n | solution.py:40
  146.8 0.0 slice-done
  146.8 0.0 slice-done.1
  146.8 0.0 copy-start.4
  146.8 5.5 %fusion.28 = f32[5,128,8,256]{1,3,2,0:T(8,128)S(1)} fusion(f32[5,128,8,256]{1,3,2,0:T(8,128)S(1)} %bitcast.52, f32[5,128,9,256]{1,3,2,0:T(8,128)} %fusion.17), kind=kLoop, calls=%fused_computation.53 | loop fusion | flops 2621440 | bytes 20971520 | tf_op jit(solution)/shard_map/sub | solution.py:45
  152.3 0.0 copy-done.4
  152.3 0.0 copy-start.7
  152.3 0.0 copy-start.8
  152.3 6.4 %fusion.58 = (bf16[5,128,2048]{1,2,0:T(8,128)(2,1)}, f32[5,128,2048]{1,2,0:T(8,128)}) fusion(f32[5,128,2048]{1,2,0:T(8,128)S(1)} %bitcast.55, f32[128,128]{1,0:T(8,128)S(1)} %copy-done.4), kind=kOutput, calls=%fused_computation.87 | convolution fusion | flops 2014576640 | bytes 13172736 | tf_op jit(solution)/shard_map/km,fmc->fkc/dot_general | solution.py:71
  158.7 4.1 %gather_fusion = bf16[16,5,128,128]{2,3,1,0:T(8,128)(2,1)} fusion(bf16[5,128,16,128]{1,3,2,0:T(8,128)(2,1)} %bitcast.57, s32[1024]{0:T(1024)S(1)} %pad_clamp_fusion), kind=kCustom, calls=%fused_computation | custom fusion | bytes 5242944 | tf_op jit(solution)/shard_map/jit(_take)/gather | solution.py:49
  162.9 0.0 copy-done
  162.9 13.2 %fusion.38 = f32[16,128,128]{1,2,0:T(8,128)} fusion(f32[2048]{0:T(1024)S(1)} %copy-done.8, bf16[5,128,2048,1]{2,1,0,3:T(8,128)(2,1)S(1)} %bitcast.50, bf16[16,5,128,128]{2,3,1,0:T(8,128)(2,1)} %gather_fusion, pred[16]{0:T(512)(128)(4,1)S(1)} %maximum_compare_fusion, bf16[2048,128]{1,0:T(8,128)(2,1)S(1)} %copy-done.7), kind=kOutput, calls=%fused_computation.63 | convolution fusion | flops 6485704704 | bytes 6823952 | tf_op jit(solution)/shard_map/kch,hl->klc/dot_general | solution.py:54
  176.1 2.6 %copy.73 = f32[16,128,128]{2,0,1:T(8,128)} copy(f32[16,128,128]{1,2,0:T(8,128)} %fusion.38) | data formatting | bytes 2097152 | tf_op jit(solution)/shard_map/kch,hl->klc/transpose | solution.py:54
  178.7 2.8 %convolution_bitcast_fusion.1 = f32[128,16,128]{2,1,0:T(8,128)} fusion(f32[16,128,128]{2,0,1:T(8,128)} %copy.73, s32[16]{0:T(128)S(1)} %bitcast.60), kind=kOutput, calls=%fused_computation.62 | convolution fusion | flops 50331904 | bytes 2097216 | tf_op jit(solution)/shard_map/bs,slc->lbc/dot_general | solution.py:59
  181.5 2.6 %copy.74 = f32[128,16,128]{0,2,1:T(8,128)} copy(f32[128,16,128]{2,1,0:T(8,128)} %convolution_bitcast_fusion.1) | data formatting | bytes 2097152 | tf_op jit(solution)/shard_map/bs,slc->lbc/transpose | solution.py:59
  184.1 2.5 %slice.120 = f32[4,128,2048]{1,2,0:T(8,128)S(1)} slice(f32[5,128,2048]{1,2,0:T(8,128)} %get-tuple-element.12), slice={[1:5], [0:128], [0:2048]} | slice | bytes 8388608 | tf_op jit(solution)/shard_map/slice | solution.py:82
  186.6 0.0 copy-done.2
  186.6 1.6 slice_add_fusion
  188.2 2.7 %pad_maximum_fusion.8 = f32[5,128,2048]{1,2,0:T(8,128)} fusion(f32[4,128,2048]{1,2,0:T(8,128)S(1)} %slice.120, f32[1,128,2048]{1,2,0:T(8,128)S(1)} %slice_add_fusion), kind=kLoop, calls=%fused_computation.56 | loop fusion | flops 1310720 | bytes 10485760 | tf_op jit(solution)/shard_map/concatenate | solution.py:82
  190.9 6.1 %copy.75 = f32[5,128,8,256]{3,2,1,0:T(8,128)} copy(f32[5,128,8,256]{1,3,2,0:T(8,128)} %bitcast.56) | data formatting | bytes 10485760 | tf_op jit(solution)/shard_map/reshape | solution.py:83
  (16 shorter events, 0.0 us)
Async XLA Ops:
  0.0 162.9 %copy-start = (bf16[640,2048]{1,0:T(8,128)(2,1)S(1)}, bf16[640,2048]{1,0:T(8,128)(2,1)}, u32[]{:S(2)}) copy-start(bf16[640,2048]{1,0:T(8,128)(2,1)} %param.12) | copy-start | bytes 7864324
  0.0 13.2 %slice-start.4 = ((f32[128,8,256]{2,1,0:T(8,128)}), f32[128,1,256]{2,1,0:T(1,128)S(1)}, s32[]{:S(2)}) async-start(f32[128,8,256]{2,1,0:T(8,128)} %param.9), calls=%async_computation.4 | async-start | bytes 262144 | tf_op jit(solution)/shard_map/slice | solution.py:64
  0.0 15.1 %copy-start.3 = (f32[128,8,256]{2,1,0:T(8,128)S(1)}, f32[128,8,256]{2,1,0:T(8,128)}, u32[]{:S(2)}) copy-start(f32[128,8,256]{2,1,0:T(8,128)} %param.9) | copy-start | bytes 3145732
  6.4 47.6 %collective-permute-start.1 = (f32[5,128,2,256]{3,1,2,0:T(8,128)}, f32[5,128,2,256]{3,1,2,0:T(8,128)}, u32[]{:S(2)}, u32[]{:S(2)}) collective-permute-start(f32[5,128,2,256]{3,1,2,0:T(8,128)} %copy.77), channel_id=1, source_target_pairs={{0,1},{1,2},{2,3},{3,4},{4,5},{5,6},{6,7},{7,8},{8,9},{9,10},{10,1... | collective-permute-start | bytes 3932168 | tf_op jit(solution)/shard_map/ppermute | solution.py:22
  9.5 47.2 %collective-permute-start.2 = (f32[5,128,2,256]{3,1,2,0:T(8,128)}, f32[5,128,2,256]{3,1,2,0:T(8,128)}, u32[]{:S(2)}, u32[]{:S(2)}) collective-permute-start(f32[5,128,2,256]{3,1,2,0:T(8,128)} %copy.78), channel_id=1, source_target_pairs={{1,0},{2,1},{3,2},{4,3},{5,4},{6,5},{7,6},{8,7},{9,8},{10,9},{11,1... | collective-permute-start | bytes 3932168 | tf_op jit(solution)/shard_map/ppermute | solution.py:23
  13.2 26.7 %collective-permute-start = (f32[128,1,256]{2,0,1:T(8,128)S(1)}, f32[128,1,256]{2,0,1:T(8,128)S(1)}, u32[]{:S(2)}, u32[]{:S(2)}) collective-permute-start(f32[128,1,256]{2,0,1:T(8,128)S(1)} %copy.81), channel_id=1, source_target_pairs={{1,0},{2,1},{3,2},{4,3},{5,4},{6,5},{7,6},{8,7},{9,8},{10,9},{11,1... | collective-permute-start | bytes 393224 | tf_op jit(solution)/shard_map/ppermute | solution.py:12
  59.7 17.8 %slice-start.2 = ((s8[5242880]{0:T(1024)(128)(4,1)}), s8[4194304]{0:T(1024)(128)(4,1)S(1)}, s32[]{:S(2)}) async-start(s8[5242880]{0:T(1024)(128)(4,1)} %bitcast.53), calls=%async_computation.2 | async-start | bytes 8388608
  68.8 8.7 %slice-start.3 = ((s8[5242880]{0:T(1024)(128)(4,1)}), s8[1048576]{0:T(1024)(128)(4,1)S(1)}, s32[]{:S(2)}) async-start(s8[5242880]{0:T(1024)(128)(4,1)} %bitcast.53), calls=%async_computation.3 | async-start | bytes 2097152
  83.0 2.4 %copy-start.1 = (f32[5,128,8,256]{1,3,2,0:T(8,128)}, f32[5,128,8,256]{1,3,2,0:T(8,128)S(1)}, u32[]{:S(2)}) copy-start(f32[5,128,8,256]{1,3,2,0:T(8,128)S(1)} %fusion.29) | copy-start | bytes 15728644
  85.3 13.2 %copy-start.5 = (f32[8,256]{1,0:T(8,128)S(1)}, f32[8,256]{1,0:T(8,128)}, u32[]{:S(2)}) copy-start(f32[8,256]{1,0:T(8,128)} %param.10) | copy-start | bytes 24580
  85.3 13.2 %copy-start.6 = (s32[1,16]{1,0:T(1,128)S(1)}, s32[1,16]{1,0:T(1,128)}, u32[]{:S(2)}) copy-start(s32[1,16]{1,0:T(1,128)} %param.11) | copy-start | bytes 196
  89.8 33.4 %collective-permute-start.3 = (f32[5,128,2,256]{3,1,2,0:T(8,128)}, f32[5,128,2,256]{3,1,2,0:T(8,128)}, u32[]{:S(2)}, u32[]{:S(2)}) collective-permute-start(f32[5,128,2,256]{3,1,2,0:T(8,128)} %copy.67), channel_id=1, source_target_pairs={{0,1},{1,2},{2,3},{3,4},{4,5},{5,6},{6,7},{7,8},{8,9},{9,10},{10,1... | collective-permute-start | bytes 3932168 | tf_op jit(solution)/shard_map/ppermute | solution.py:22
  94.5 31.5 %collective-permute-start.4 = (f32[5,128,2,256]{3,1,2,0:T(8,128)}, f32[5,128,2,256]{3,1,2,0:T(8,128)}, u32[]{:S(2)}, u32[]{:S(2)}) collective-permute-start(f32[5,128,2,256]{3,1,2,0:T(8,128)} %copy.69), channel_id=1, source_target_pairs={{1,0},{2,1},{3,2},{4,3},{5,4},{6,5},{7,6},{8,7},{9,8},{10,9},{11,1... | collective-permute-start | bytes 3932168 | tf_op jit(solution)/shard_map/ppermute | solution.py:23
  129.0 17.8 %slice-start = ((s8[5242880]{0:T(1024)(128)(4,1)}), s8[4194304]{0:T(1024)(128)(4,1)S(1)}, s32[]{:S(2)}) async-start(s8[5242880]{0:T(1024)(128)(4,1)} %bitcast.51), calls=%async_computation | async-start | bytes 8388608
  138.1 8.7 %slice-start.1 = ((s8[5242880]{0:T(1024)(128)(4,1)}), s8[1048576]{0:T(1024)(128)(4,1)S(1)}, s32[]{:S(2)}) async-start(s8[5242880]{0:T(1024)(128)(4,1)} %bitcast.51), calls=%async_computation.1 | async-start | bytes 2097152
  146.8 5.5 %copy-start.4 = (f32[128,128]{1,0:T(8,128)S(1)}, f32[128,128]{1,0:T(8,128)}, u32[]{:S(2)}) copy-start(f32[128,128]{1,0:T(8,128)} %param.15) | copy-start | bytes 196612
  152.3 10.6 %copy-start.7 = (bf16[2048,128]{1,0:T(8,128)(2,1)S(1)}, bf16[2048,128]{1,0:T(8,128)(2,1)}, u32[]{:S(2)}) copy-start(bf16[2048,128]{1,0:T(8,128)(2,1)} %param.14) | copy-start | bytes 1572868
  152.3 10.5 %copy-start.8 = (f32[2048]{0:T(1024)S(1)}, f32[2048]{0:T(1024)}, u32[]{:S(2)}) copy-start(f32[2048]{0:T(1024)} %param.13) | copy-start | bytes 24580
  184.1 2.6 %copy-start.2 = (f32[128,16,128]{0,2,1:T(8,128)S(1)}, f32[128,16,128]{0,2,1:T(8,128)}, u32[]{:S(2)}) copy-start(f32[128,16,128]{0,2,1:T(8,128)} %copy.74) | copy-start | bytes 3145732
where the time goes:
time: 198 us; the launch traced here: 197 us
  local copies, waits for them, and re-layouts  63.8 us (32%)
  other arithmetic  55.2 us (28%)
  waiting for transfers between devices  42 us (21%)
  matrix products  22.3 us (11%)
  starting transfers between devices  13.4 us (7%)
    ppermute x2, waiting for transfers between devices, padded_2(): before = lax.ppermute(last, axis, up)  24.7 us
    mul x2, other arithmetic, min_mod(): 0.5 * (jnp.sign(left) + jnp.sign(right))  18.2 us
    select_n x2, other arithmetic, advance(): jnp.where(speed > 0.0, speed * (upper_q + 0.5 * (1.0 - speed) * upper_s),...  17.4 us
    ppermute x1, waiting for transfers between devices, shifted(): return lax.ppermute(block, axis, route)  17.3 us
    dot_general x1, matrix products, radiate(): jnp.einsum('kch,hl->klc', hidden, w_second, preferred_element_type=jnp.fl...  13.2 us
    unnamed x32, local copies, waits for them, and re-layouts  12.3 us
    sub x2, other arithmetic, advance(): return padded[:, :, 2:length + 2] - (fluxes[:, :, 1:] - fluxes[:, :, :-1])  11 us
    slice x3, local copies, waits for them, and re-layouts, padded_2(): last = lax.slice_in_dim(x, length - width, length, axis=dim)  9.69 us
  transfers between devices with their start and end apart: 5, of which 2 were waited for; matrix products, arithmetic and copies ran while one was open for 16% of the time, Pallas kernels for 0%

commit v1 on v0

v1 whole, which is shorter than its diff:
```python
import functools

import jax
import jax.numpy as jnp
from jax import lax
from jax.experimental import pallas as pl
from jax.experimental.pallas import tpu as pltpu
from jax.sharding import PartitionSpec as P

STEPS = 2
REACH = 2 * STEPS
SCALE = 4096.0
PARTS = 2
CHUNKS = 4
MIB = 1 << 20


def pack_kernel(state_ref, wind_ref, up_ref, down_ref):
    fields, levels, rows, lons = state_ref.shape
    flat = state_ref.reshape(fields * levels * rows, lons)
    winds = wind_ref.reshape(levels * rows, lons)
    for k in range(REACH):
        for f in range(fields):
            base = f * levels * rows
            up_ref[0, k * fields + f] = flat[pl.ds(base + rows - REACH + k, levels, stride=rows), :] * SCALE
            down_ref[0, k * fields + f] = flat[pl.ds(base + k, levels, stride=rows), :] * SCALE
    for k in range(2):
        up_ref[0, REACH * fields + k] = winds[pl.ds(rows - 2 + k, levels, stride=rows), :] * SCALE
    for k in range(3):
        down_ref[0, REACH * fields + k] = winds[pl.ds(k, levels, stride=rows), :] * SCALE


def pack(state, wind):
    fields, levels, rows, lons = state.shape
    part = lons // PARTS
    step = levels // CHUNKS
    slabs = REACH * fields
    return pl.pallas_call(
        pack_kernel,
        grid=(PARTS, CHUNKS),
        in_specs=[
            pl.BlockSpec((fields, step, rows, part), lambda h, i: (0, i, 0, h)),
            pl.BlockSpec((step, rows, part), lambda h, i: (i, 0, h)),
        ],
        out_specs=[
            pl.BlockSpec((1, slabs + 2, step, part), lambda h, i: (h, 0, i, 0)),
            pl.BlockSpec((1, slabs + 3, step, part), lambda h, i: (h, 0, i, 0)),
        ],
        out_shape=[
            jax.ShapeDtypeStruct((PARTS, slabs + 2, levels, part), jnp.float32),
            jax.ShapeDtypeStruct((PARTS, slabs + 3, levels, part), jnp.float32),
        ],
        name="pack",
        compiler_params=pltpu.CompilerParams(vmem_limit_bytes=40 * MIB),
        cost_estimate=pl.CostEstimate(flops=10**6, bytes_accessed=12 * 10**6, transcendentals=0),
    )(state, wind)


def limited(left, right):
    return jnp.maximum(jnp.minimum(left, right), 0.0) + jnp.minimum(jnp.maximum(left, right), 0.0)


def advance(q, c, ck, positive, first, last):
    diff = {j: q[j + 1] - q[j] for j in range(first - 2, last + 2)}
    slope = {j: limited(diff[j], diff[j - 1]) for j in range(first - 1, last + 2)}
    flux = {}
    for j in range(first, last + 2):
        flux[j] = c[j] * jnp.where(positive[j], q[j - 1], q[j]) + ck[j] * jnp.where(
            positive[j], slope[j - 1], slope[j]
        )
    return {j: q[j] - (flux[j + 1] - flux[j]) for j in range(first, last + 1)}


def gelu(v):
    inner = v * (0.7978845608028654 + (0.7978845608028654 * 0.044715) * (v * v))
    half = 0.5 * v
    return (half + half * jnp.tanh(inner)).astype(jnp.bfloat16)


def main_kernel(part, flags, state_ref, wind_ref, north_ref, south_ref, sun_ref, bias_ref,
                remap_ref, w1_hbm, w2_hbm, *rest):
    out_ref, adv, x16, w1, w2, sems = rest[-6:]
    step_id = pl.program_id(0)
    fields, chunk, rows, lons = state_ref.shape
    levels = adv.shape[2]
    slabs = REACH * fields
    load_1 = pltpu.make_async_copy(w1_hbm, w1, sems.at[0])
    load_2 = pltpu.make_async_copy(w2_hbm, w2, sems.at[1])

    @pl.when(step_id == 0)
    def _():
        load_1.start()
        load_2.start()

    @pl.when(step_id < CHUNKS)
    def _():
        flat = state_ref.reshape(fields * chunk * rows, lons)
        winds = wind_ref.reshape(chunk * rows, lons)
        inner = jnp.where(flags[flags.shape[0] - 1] > 0, 1.0, 0.0)

        @pl.loop(0, chunk // 8)
        def _(t):
            here = pl.ds(pl.multiple_of(t * 8, 8), 8)
            there = pl.ds(pl.multiple_of(step_id * chunk + t * 8, 8), 8)
            c = {}
            for j in range(-2, rows + 3):
                if j < 0:
                    c[j] = north_ref[slabs + 2 + j, here, :]
                elif j < rows:
                    c[j] = winds[pl.ds(t * 8 * rows + j, 8, stride=rows), :]
                else:
                    c[j] = south_ref[slabs + j - rows, here, :]
            positive = {j: v > 0.0 for j, v in c.items()}
            ck = {j: 0.5 * (jnp.abs(v) - v * v) for j, v in c.items()}
            for f in range(fields):
                q = {}
                for j in range(-REACH, rows + REACH):
                    if j < 0:
                        q[j] = north_ref[(j + REACH) * fields + f, here, :]
                    elif j < rows:
                        q[j] = flat[pl.ds(f * chunk * rows + t * 8 * rows + j, 8, stride=rows), :]
                    else:
                        q[j] = south_ref[(j - rows) * fields + f, here, :]
                q = advance(q, c, ck, positive, -2, rows + 1)
                q[-1] = q[-1] * inner
                q[-2] = q[-2] * inner
                q = advance(q, c, ck, positive, 0, rows - 1)
                for j in range(rows):
                    adv[j, f, there, :] = q[j]

    @pl.when(step_id == CHUNKS)
    def _():
        load_1.wait()
        load_2.wait()
        flat_out = out_ref.reshape(fields * levels * rows, lons)
        remap = remap_ref[...]
        r_high = remap.astype(jnp.bfloat16)
        r_low = (remap - r_high.astype(jnp.float32)).astype(jnp.bfloat16)
        r_all = jnp.concatenate([r_high, r_low, r_high], axis=1)
        hidden_size = w1.shape[0]
        tile = hidden_size // 4

        for pair in range(rows // 2):
            a, b = 2 * pair, 2 * pair + 1
            for f in range(fields):
                x = jnp.concatenate([adv[a, f], adv[b, f]], axis=1)
                high = x.astype(jnp.bfloat16)
                low = (x - high.astype(jnp.float32)).astype(jnp.bfloat16)
                stacked = jnp.concatenate([high, high, low], axis=0)
                y = jnp.dot(r_all, stacked, preferred_element_type=jnp.float32)
                x16[pl.ds(f * levels, levels), :] = y.astype(jnp.bfloat16)
                flat_out[pl.ds(f * levels * rows + a, levels, stride=rows), :] = y[:, :lons]
                flat_out[pl.ds(f * levels * rows + b, levels, stride=rows), :] = y[:, lons:]
            lit_a = flags[PARTS * a + part]
            lit_b = flags[PARTS * b + part]

            @pl.when(lit_a + lit_b > 0)
            def _():
                inputs = x16[...]

                def layer(t):
                    z = jnp.dot(w1[pl.ds(t * tile, tile), :], inputs,
                                preferred_element_type=jnp.float32)
                    wide = bias_ref[pl.ds(t * tile, tile), :]
                    return z + jnp.concatenate([wide, wide], axis=1)

                net = jnp.zeros((levels, 2 * lons), jnp.float32)
                z = layer(0)
                for t in range(4):
                    later = layer(t + 1) if t < 3 else None
                    net = net + jnp.dot(w2[:, pl.ds(t * tile, tile)], gelu(z),
                                        preferred_element_type=jnp.float32)
                    z = later
                for r, lit, values in ((a, lit_a, net[:, :lons]), (b, lit_b, net[:, lons:])):
                    weight = sun_ref[pl.ds(r, 1), :] * jnp.where(lit > 0, 1.0, 0.0)
                    place = pl.ds(r, levels, stride=rows)
                    flat_out[place, :] = flat_out[place, :] + weight * values


def compute(part, flags, state, wind, north, south, sunlight, bias, remap, w1, w2, before):
    fields, levels, rows, lons = state.shape
    width = lons // PARTS
    step = levels // CHUNKS
    last = CHUNKS - 1
    hidden_size = w1.shape[0]
    any_spec = pl.BlockSpec(memory_space=pl.ANY)
    in_specs = [
        pl.BlockSpec((fields, step, rows, width), lambda i, s: (0, jnp.minimum(i, last), 0, part)),
        pl.BlockSpec((step, rows, width), lambda i, s: (jnp.minimum(i, last), 0, part)),
        pl.BlockSpec((north.shape[0], step, width), lambda i, s: (0, jnp.minimum(i, last), 0)),
        pl.BlockSpec((south.shape[0], step, width), lambda i, s: (0, jnp.minimum(i, last), 0)),
        pl.BlockSpec((rows, width), lambda i, s: (0, part)),
        pl.BlockSpec((hidden_size, width), lambda i, s: (0, 0)),
        pl.BlockSpec((levels, levels), lambda i, s: (0, 0)),
        any_spec,
        any_spec,
    ]
    operands = [flags, state, wind, north, south, sunlight, bias, remap, w1, w2]
    aliases = {}
    if before is not None:
        in_specs.append(any_spec)
        operands.append(before)
        aliases = {len(operands) - 1: 0}
    return pl.pallas_call(
        functools.partial(main_kernel, part),
        grid_spec=pltpu.PrefetchScalarGridSpec(
            num_scalar_prefetch=1,
            grid=(CHUNKS + 1,),
            in_specs=in_specs,
            out_specs=pl.BlockSpec((fields, levels, rows, width), lambda i, s: (0, 0, 0, part)),
            scratch_shapes=[
                pltpu.VMEM((rows, fields, levels, width), jnp.float32),
                pltpu.VMEM((fields * levels, 2 * width), jnp.bfloat16),
                pltpu.VMEM(w1.shape, jnp.bfloat16),
                pltpu.VMEM(w2.shape, jnp.bfloat16),
                pltpu.SemaphoreType.DMA((2,)),
            ],
        ),
        out_shape=jax.ShapeDtypeStruct(state.shape, jnp.float32),
        input_output_aliases=aliases,
        name="column_step",
        compiler_params=pltpu.CompilerParams(vmem_limit_bytes=48 * MIB),
        cost_estimate=pl.CostEstimate(flops=4 * 10**9, bytes_accessed=12 * 10**6, transcendentals=2 * 10**6),
    )(*operands)


def shards(state, wind, sunlight, day_list, w_first, bias, w_second, remap):
    count = lax.axis_size("lat")
    upward = [(i, i + 1) for i in range(count - 1)]
    downward = [(i + 1, i) for i in range(count - 1)]
    up, down = pack(state, wind)
    halos = []
    for part in range(PARTS):
        north = lax.ppermute(up[part].astype(jnp.float16), "lat", upward)
        south = lax.ppermute(down[part].astype(jnp.float16), "lat", downward)
        halos.append((north, south))
    blocks = day_list.shape[1]
    block_ids = jnp.arange(blocks, dtype=jnp.int32)
    lit = jnp.any(day_list[0][None, :] == block_ids[:, None], axis=1).astype(jnp.int32)
    inner = (lax.axis_index("lat") > 0).astype(jnp.int32)
    flags = jnp.concatenate([lit, inner[None]])
    w1, w2 = w_first.T, w_second.T
    wide_bias = jnp.broadcast_to(bias[:, None], (bias.shape[0], state.shape[3] // PARTS))
    out = None
    for part in range(PARTS):
        north, south = [h.astype(jnp.float32) * (1.0 / SCALE) for h in halos[part]]
        out = compute(part, flags, state, wind, north, south, sunlight, wide_bias, remap, w1, w2, out)
    return out


def solution(mesh):
    placed = (
        P("member", None, "lat", None),
        P("member", "lat", None),
        P(("member", "lat"), None),
        P(("member", "lat"), None),
        P(),
        P(),
        P(),
        P(),
    )
    return jax.shard_map(
        shards,
        mesh=mesh,
        in_specs=placed,
        out_specs=P("member", None, "lat", None),
        check_vma=False,
    )
```

time: 198 us -> 80.6 us (0.41)
  the two profiles are of different devices: /device:TPU:20 before, /device:TPU:1 now
where the time goes in v1:
time: 80.6 us; the launch traced here: 80.1 us
  Pallas kernels  33.1 us (41%)
  waiting for transfers between devices  17.9 us (22%)
  starting transfers between devices  11.6 us (14%)
  local copies, waits for them, and re-layouts  11.1 us (14%)
  other arithmetic  5.99 us (7%)
    pallas_call x2, Pallas kernels, compute(): pl.pallas_call(functools.partial(main_kernel, part), grid_spec=pltpu.Pref...  30.9 us
    ppermute x2, waiting for transfers between devices, shards(): north = lax.ppermute(up[part].astype(jnp.float16), 'lat', upward)  17.9 us
    unnamed x18, local copies, waits for them, and re-layouts  7.61 us
    ppermute x2, starting transfers between devices, shards(): north = lax.ppermute(up[part].astype(jnp.float16), 'lat', upward)  6.45 us
    ppermute x2, starting transfers between devices, shards(): south = lax.ppermute(down[part].astype(jnp.float16), 'lat', downward)  5.19 us
    mul x4, other arithmetic, shards(): north, south = [h.astype(jnp.float32) * (1.0 / SCALE) for h in halos[part]]  5.18 us
    pallas_call x1, Pallas kernels, pack(): pl.pallas_call(pack_kernel, grid=(PARTS, CHUNKS), in_specs=[pl.BlockSpec(...  2.18 us
    convert_element_type x1, local copies, waits for them, and re-layouts, shards(): south = lax.ppermute(down[part].astype(jnp.float16), 'lat', downward)  1.68 us
  transfers between devices with their start and end apart: 4, of which 1 were waited for; matrix products, arithmetic and copies ran while one was open for 13% of the time, Pallas kernels for 19%

profile of v1, /device:TPU:1, one launch (start us, length us, event | category | flops | bytes accessed | tf_op | source)
XLA Modules:
  0.0 80.1 jit_solution(11319848372453560278)
XLA Ops:
  0.0 0.0 copy-start
  0.0 2.5 %copy-done = f32[5,128,8,256]{3,2,1,0:T(8,128)S(1)} copy-done((f32[5,128,8,256]{3,2,1,0:T(8,128)S(1)}, f32[5,128,8,256]{3,2,1,0:T(8,128)}, u32[]{:S(2)}) %copy-start) | copy-done | bytes 5242904
  2.5 0.0 copy-start.1
  2.5 1.2 %copy-done.1 = f32[128,8,256]{2,1,0:T(8,128)S(1)} copy-done((f32[128,8,256]{2,1,0:T(8,128)S(1)}, f32[128,8,256]{2,1,0:T(8,128)}, u32[]{:S(2)}) %copy-start.1) | copy-done | bytes 1048600
  3.7 2.2 %pack.1 = (f32[2,22,128,128]{3,2,1,0:T(8,128)S(1)}, f32[2,23,128,128]{3,2,1,0:T(8,128)S(1)}) custom-call(f32[5,128,8,256]{3,2,1,0:T(8,128)S(1)} %copy-done, f32[128,8,256]{2,1,0:T(8,128)S(1)} %copy-done.1), custom_call_target="tpu_custom_call" | custom-call | flops 1000000 | bytes 12000000 | tf_op jit(solution)/shard_map/pack/pallas_call | solution.py:38
  5.9 0.3 convert.10
  6.2 1.5 %slice_bitcast_fusion.2 = (f16[22,128,128]{2,1,0:T(8,128)(2,1)}, f16[22,128,128]{2,1,0:T(8,128)(2,1)}) fusion(f16[2,22,128,128]{3,2,1,0:T(8,128)(2,1)S(1)} %convert.10), kind=kLoop, calls=%fused_computation.6 | loop fusion | bytes 2883584 | tf_op jit(solution)/shard_map/convert_element_type | solution.py:234
  7.7 4.5 %collective-permute-start.2 = (f16[22,128,128]{2,1,0:T(8,128)(2,1)}, f16[22,128,128]{2,1,0:T(8,128)(2,1)}, u32[]{:S(2)}, u32[]{:S(2)}) collective-permute-start(f16[22,128,128]{2,1,0:T(8,128)(2,1)} %get-tuple-element.11), channel_id=1, source_target_pairs={{0,1},{1,2},{2,3},{3,4},{4,5},{5,6},{6,7},{7,8},{8,9},{9,10},{10,1... | collective-permute-start | bytes 2162696 | tf_op jit(solution)/shard_map/ppermute | solution.py:234
  12.2 1.9 %collective-permute-start = (f16[22,128,128]{2,1,0:T(8,128)(2,1)}, f16[22,128,128]{2,1,0:T(8,128)(2,1)}, u32[]{:S(2)}, u32[]{:S(2)}) collective-permute-start(f16[22,128,128]{2,1,0:T(8,128)(2,1)} %get-tuple-element.12), channel_id=1, source_target_pairs={{0,1},{1,2},{2,3},{3,4},{4,5},{5,6},{6,7},{7,8},{8,9},{9,10},{10,1... | collective-permute-start | bytes 2162696 | tf_op jit(solution)/shard_map/ppermute | solution.py:234
  14.1 0.3 convert.11
  14.5 0.0 copy-start.5
  14.5 1.7 %slice_bitcast_fusion = (f16[23,128,128]{2,1,0:T(8,128)(2,1)}, f16[23,128,128]{2,1,0:T(8,128)(2,1)}) fusion(f16[2,23,128,128]{3,2,1,0:T(8,128)(2,1)S(1)} %convert.11), kind=kLoop, calls=%fused_computation.4 | loop fusion | bytes 3014656 | tf_op jit(solution)/shard_map/convert_element_type | solution.py:235
  16.2 3.3 %collective-permute-start.3 = (f16[23,128,128]{2,1,0:T(8,128)(2,1)}, f16[23,128,128]{2,1,0:T(8,128)(2,1)}, u32[]{:S(2)}, u32[]{:S(2)}) collective-permute-start(f16[23,128,128]{2,1,0:T(8,128)(2,1)} %get-tuple-element.9), channel_id=1, source_target_pairs={{1,0},{2,1},{3,2},{4,3},{5,4},{6,5},{7,6},{8,7},{9,8},{10,9},{11,1... | collective-permute-start | bytes 2261000 | tf_op jit(solution)/shard_map/ppermute | solution.py:235
  19.4 1.9 %collective-permute-start.1 = (f16[23,128,128]{2,1,0:T(8,128)(2,1)}, f16[23,128,128]{2,1,0:T(8,128)(2,1)}, u32[]{:S(2)}, u32[]{:S(2)}) collective-permute-start(f16[23,128,128]{2,1,0:T(8,128)(2,1)} %get-tuple-element.10), channel_id=1, source_target_pairs={{1,0},{2,1},{3,2},{4,3},{5,4},{6,5},{7,6},{8,7},{9,8},{10,9},{11,1... | collective-permute-start | bytes 2261000 | tf_op jit(solution)/shard_map/ppermute | solution.py:235
  21.4 1.2 %copy.13 = bf16[2048,128]{0,1:T(8,128)(2,1)S(1)} copy(bf16[2048,128]{1,0:T(8,128)(2,1)} %param.14) | data formatting | bytes 1048576 | tf_op args[6]
  22.6 0.0 copy-done.5
  22.6 0.0 copy-start.7
  22.7 2.6 %copy.12 = bf16[640,2048]{0,1:T(8,128)(2,1)} copy(bf16[640,2048]{1,0:T(8,128)(2,1)S(1)} %copy-done.5) | data formatting | bytes 5242880 | tf_op args[4]
  25.3 0.0 copy-done.7
  25.3 0.1 fusion
  25.4 0.1 add_convert_fusion.flags
  25.5 0.0 collective-permute-done.2
  25.5 1.3 %convert_multiply_fusion.2.north_ref = f32[22,128,128]{2,1,0:T(8,128)S(1)} fusion(f16[22,128,128]{2,1,0:T(8,128)(2,1)} %collective-permute-done.2), kind=kLoop, calls=%fused_computation.2 | loop fusion | flops 720896 | bytes 2162688 | tf_op jit(solution)/shard_map/mul | solution.py:246
  26.7 17.9 %collective-permute-done = f16[22,128,128]{2,1,0:T(8,128)(2,1)} collective-permute-done((f16[22,128,128]{2,1,0:T(8,128)(2,1)}, f16[22,128,128]{2,1,0:T(8,128)(2,1)}, u32[]{:S(2)}, u32[]{:S(2)}) %collective-permute-start) | collective-permute-done | bytes 720928 | tf_op jit(solution)/shard_map/ppermute | solution.py:234
  44.6 1.3 %convert_multiply_fusion.3.north_ref = f32[22,128,128]{2,1,0:T(8,128)S(1)} fusion(f16[22,128,128]{2,1,0:T(8,128)(2,1)} %collective-permute-done), kind=kLoop, calls=%fused_computation.3 | loop fusion | flops 720896 | bytes 2162688 | tf_op jit(solution)/shard_map/mul | solution.py:246
  45.9 0.0 copy-start.6
  45.9 0.0 copy-start.2
  45.9 0.0 copy-start.3
  45.9 0.0 copy-start.4
  45.9 0.0 collective-permute-done.3
  45.9 1.4 %convert_multiply_fusion.south_ref = f32[23,128,128]{2,1,0:T(8,128)S(1)} fusion(f16[23,128,128]{2,1,0:T(8,128)(2,1)} %collective-permute-done.3), kind=kLoop, calls=%fused_computation | loop fusion | flops 753664 | bytes 2260992 | tf_op jit(solution)/shard_map/mul | solution.py:246
  47.3 0.0 copy-done.6
  47.3 0.3 broadcast_in_dim.12.bias_ref
  47.7 0.0 copy-done.2
  47.7 0.0 copy-done.3
  47.7 0.0 copy-done.4
  47.7 15.4 %column_step.2.rest_0_ = f32[5,128,8,256]{3,2,1,0:T(8,128)} custom-call(s32[17]{0:T(128)S(1)} %add_convert_fusion.flags, f32[5,128,8,256]{3,2,1,0:T(8,128)} %state_ref.5, f32[128,8,256]{2,1,0:T(8,128)S(1)} %copy-done.2, f32[22,128,128]{2,1,0:T(8,128)S(1)} %convert_multiply_fusion.2.north_ref, f32[23,128,128]{2,1,0:T(8,128)S(1)} %convert_multiply_fusion.south_ref, ...), custom_call_target="tpu_custom_call" | custom-call | flops 4000000000 | bytes 12000000 | tf_op jit(solution)/shard_map/column_step/pallas_call | solution.py:204
  63.1 0.0 collective-permute-done.1
  63.1 1.3 %convert_multiply_fusion.1.south_ref = f32[23,128,128]{2,1,0:T(8,128)S(1)} fusion(f16[23,128,128]{2,1,0:T(8,128)(2,1)} %collective-permute-done.1), kind=kLoop, calls=%fused_computation.1 | loop fusion | flops 753664 | bytes 2260992 | tf_op jit(solution)/shard_map/mul | solution.py:246
  64.4 15.5 %column_step.3 = f32[5,128,8,256]{3,2,1,0:T(8,128)} custom-call(s32[17]{0:T(128)S(1)} %add_convert_fusion.flags, f32[5,128,8,256]{3,2,1,0:T(8,128)} %state_ref.5, f32[128,8,256]{2,1,0:T(8,128)S(1)} %copy-done.2, f32[22,128,128]{2,1,0:T(8,128)S(1)} %convert_multiply_fusion.3.north_ref, ...), custom_call_target="tpu_custom_call", output_to_operand_aliasing={{}: (10, {})} | custom-call | flops 4000000000 | bytes 12000000 | tf_op jit(solution)/shard_map/column_step/pallas_call | solution.py:204
Async XLA Ops:
  0.0 2.5 %copy-start = (f32[5,128,8,256]{3,2,1,0:T(8,128)S(1)}, f32[5,128,8,256]{3,2,1,0:T(8,128)}, u32[]{:S(2)}) copy-start(f32[5,128,8,256]{3,2,1,0:T(8,128)} %state_ref.5) | copy-start | bytes 15728644
  2.5 1.2 %copy-start.1 = (f32[128,8,256]{2,1,0:T(8,128)S(1)}, f32[128,8,256]{2,1,0:T(8,128)}, u32[]{:S(2)}) copy-start(f32[128,8,256]{2,1,0:T(8,128)} %wind_ref.5) | copy-start | bytes 3145732
  7.7 17.8 %collective-permute-start.2 = (f16[22,128,128]{2,1,0:T(8,128)(2,1)}, f16[22,128,128]{2,1,0:T(8,128)(2,1)}, u32[]{:S(2)}, u32[]{:S(2)}) collective-permute-start(f16[22,128,128]{2,1,0:T(8,128)(2,1)} %get-tuple-element.11), channel_id=1, source_target_pairs={{0,1},{1,2},{2,3},{3,4},{4,5},{5,6},{6,7},{7,8},{8,9},{9,10},{10,1... | collective-permute-start | bytes 2162696 | tf_op jit(solution)/shard_map/ppermute | solution.py:234
  12.2 32.4 %collective-permute-start = (f16[22,128,128]{2,1,0:T(8,128)(2,1)}, f16[22,128,128]{2,1,0:T(8,128)(2,1)}, u32[]{:S(2)}, u32[]{:S(2)}) collective-permute-start(f16[22,128,128]{2,1,0:T(8,128)(2,1)} %get-tuple-element.12), channel_id=1, source_target_pairs={{0,1},{1,2},{2,3},{3,4},{4,5},{5,6},{6,7},{7,8},{8,9},{9,10},{10,1... | collective-permute-start | bytes 2162696 | tf_op jit(solution)/shard_map/ppermute | solution.py:234
  14.5 8.2 %copy-start.5 = (bf16[640,2048]{1,0:T(8,128)(2,1)S(1)}, bf16[640,2048]{1,0:T(8,128)(2,1)}, u32[]{:S(2)}) copy-start(bf16[640,2048]{1,0:T(8,128)(2,1)} %param.12) | copy-start | bytes 7864324
  16.2 29.8 %collective-permute-start.3 = (f16[23,128,128]{2,1,0:T(8,128)(2,1)}, f16[23,128,128]{2,1,0:T(8,128)(2,1)}, u32[]{:S(2)}, u32[]{:S(2)}) collective-permute-start(f16[23,128,128]{2,1,0:T(8,128)(2,1)} %get-tuple-element.9), channel_id=1, source_target_pairs={{1,0},{2,1},{3,2},{4,3},{5,4},{6,5},{7,6},{8,7},{9,8},{10,9},{11,1... | collective-permute-start | bytes 2261000 | tf_op jit(solution)/shard_map/ppermute | solution.py:235
  19.4 43.6 %collective-permute-start.1 = (f16[23,128,128]{2,1,0:T(8,128)(2,1)}, f16[23,128,128]{2,1,0:T(8,128)(2,1)}, u32[]{:S(2)}, u32[]{:S(2)}) collective-permute-start(f16[23,128,128]{2,1,0:T(8,128)(2,1)} %get-tuple-element.10), channel_id=1, source_target_pairs={{1,0},{2,1},{3,2},{4,3},{5,4},{6,5},{7,6},{8,7},{9,8},{10,9},{11,1... | collective-permute-start | bytes 2261000 | tf_op jit(solution)/shard_map/ppermute | solution.py:235
  22.6 2.6 %copy-start.7 = (s32[1,16]{1,0:T(1,128)S(1)}, s32[1,16]{1,0:T(1,128)}, u32[]{:S(2)}) copy-start(s32[1,16]{1,0:T(1,128)} %param.11) | copy-start | bytes 196
  45.9 1.4 %copy-start.6 = (f32[2048]{0:T(1024)S(1)}, f32[2048]{0:T(1024)}, u32[]{:S(2)}) copy-start(f32[2048]{0:T(1024)} %param.13) | copy-start | bytes 24580
  45.9 1.8 %copy-start.2 = (f32[128,8,256]{2,1,0:T(8,128)S(1)}, f32[128,8,256]{2,1,0:T(8,128)}, u32[]{:S(2)}) copy-start(f32[128,8,256]{2,1,0:T(8,128)} %wind_ref.5) | copy-start | bytes 3145732
  45.9 1.8 %copy-start.3 = (f32[128,128]{1,0:T(8,128)S(1)}, f32[128,128]{1,0:T(8,128)}, u32[]{:S(2)}) copy-start(f32[128,128]{1,0:T(8,128)} %remap_ref.3) | copy-start | bytes 196612
  45.9 1.8 %copy-start.4 = (f32[8,256]{1,0:T(8,128)S(1)}, f32[8,256]{1,0:T(8,128)}, u32[]{:S(2)}) copy-start(f32[8,256]{1,0:T(8,128)} %sun_ref.3) | copy-start | bytes 24580
